TPU v7x, 32 devices: a whole 2x2x4 slice. The times are simulated.
32 devices in a mesh: section: 4 (over y, x), ctx: 8 (over z, core).
Axes of the slice: x: 2, y: 2, z: 4, core: 2. Of those that a mesh axis runs over, the one named last changes fastest.
Arguments:
- queries: bfloat16 [4, 1024, 2048], P('section', 'ctx'), may hold values from -6 to 6
- key_states: bfloat16 [4, 1024, 2048], P('section', 'ctx'), may hold values from -6 to 6
- value_states: bfloat16 [4, 1024, 2048], P('section', 'ctx'), may hold values from -6 to 6
- upstream: bfloat16 [4, 1024, 2048], P('section', 'ctx'), may hold values from -6 to 6
- layout: int32 [4, 16, 8, 4], P('section', 'ctx'), may hold values from 0 to 7, as said below
- segments: int32 [4, 8], P('section'), may hold values from 0 to 2, never falling along the last dimension, each value on 1 to 4 neighbouring positions
Outputs:
- attended: bfloat16 [4, 1024, 2048], P('section', 'ctx')
- grad_queries: bfloat16 [4, 1024, 2048], P('section', 'ctx')
- grad_keys: bfloat16 [4, 1024, 2048], P('section', 'ctx')
- grad_values: bfloat16 [4, 1024, 2048], P('section', 'ctx')
Inputs may be any that keep to these rules, and one draw needn't show every extreme that they name: `layout`: for section s, head h and query block a the four entries are a, a - 1, a - 2 and a - 3 - r for some r from 0 to 4, each taken modulo 8; they are distinct.
All inputs are finite; a program needn't handle non-finite values.
Results may differ from a plain program's by a relative error of at most 0.04.
Values may be sent and summed in bfloat16 or wider, within the bound.
A program may use at most 64 MiB of HBM per device.

v0:
```python
import math

import jax
import jax.numpy as jnp
from jax import lax
from jax.sharding import PartitionSpec as P

HEADS = 16
BLK = 128


def passed_along(value, axis, steps):
    count = lax.axis_size(axis)
    pairs = [(source, (source + steps) % count) for source in range(count)]
    return lax.ppermute(value, axis, pairs)


def gather_blocks(blocks, layout):
    head_index = jnp.arange(layout.shape[0])[:, None, None]
    picked = blocks[layout, :, head_index, :]
    return picked.reshape(
        layout.shape[0], layout.shape[1], layout.shape[2] * blocks.shape[1], blocks.shape[3]
    )


def visible_mask(layout, segments, block_rows):
    block_count = layout.shape[1]
    query_block = jnp.arange(block_count)[None, :, None]
    same_doc = segments[layout] == segments[query_block]
    earlier = layout < query_block
    position = jnp.arange(block_rows)
    within = position[None, None, None, None, :] <= position[None, None, :, None, None]
    diagonal = (layout == query_block)[:, :, None, :, None] & within
    visible = same_doc[:, :, None, :, None] & (earlier[:, :, None, :, None] | diagonal)
    return visible.reshape(layout.shape[0], block_count, block_rows, layout.shape[2] * block_rows)


def scatter_blocks(picked, layout, block_rows):
    head_count, block_count, slot_count = layout.shape
    head_dim = picked.shape[-1]
    pieces = picked.reshape(head_count, block_count, slot_count, block_rows, head_dim)
    summed = (
        pieces[:, :, 0]
        + jnp.roll(pieces[:, :, 1], -1, axis=1)
        + jnp.roll(pieces[:, :, 2], -2, axis=1)
    )
    head_offset = (jnp.arange(head_count, dtype=jnp.int32) * block_count)[:, None]
    target_ids = (layout[:, :, 3] + head_offset).reshape(head_count * block_count)
    distant = jax.ops.segment_sum(
        pieces[:, :, 3].reshape(head_count * block_count, block_rows, head_dim),
        target_ids,
        num_segments=head_count * block_count,
    )
    summed = summed + distant.reshape(head_count, block_count, block_rows, head_dim)
    return summed.transpose(1, 2, 0, 3)


def forward_part(query_blocks, key_blocks, value_blocks, layout, segments):
    score_scale = 1.0 / math.sqrt(query_blocks.shape[-1])
    key_rows = gather_blocks(key_blocks, layout)
    value_rows = gather_blocks(value_blocks, layout)
    visible = visible_mask(layout, segments, query_blocks.shape[1])
    scores = (
        jnp.einsum("aihd,hamd->haim", query_blocks, key_rows, preferred_element_type=jnp.float32)
        * score_scale
    )
    scores = jnp.where(visible, scores, -jnp.inf)
    row_max = jnp.max(scores, axis=-1, keepdims=True)
    raised = jnp.exp(scores - row_max)
    weights = raised / jnp.sum(raised, axis=-1, keepdims=True)
    weights_low = weights.astype(jnp.bfloat16)
    attended = jnp.einsum(
        "haim,hamd->aihd", weights_low, value_rows, preferred_element_type=jnp.float32
    ).astype(jnp.bfloat16)
    return (attended, weights, weights_low, key_rows, value_rows)


def backward_part(
    query_blocks, grad_blocks, attended, weights, weights_low, key_rows, value_rows, layout
):
    score_scale = 1.0 / math.sqrt(query_blocks.shape[-1])
    block_rows = query_blocks.shape[1]
    grad_weight = jnp.einsum(
        "aihd,hamd->haim", grad_blocks, value_rows, preferred_element_type=jnp.float32
    )
    row_inner = jnp.sum(grad_blocks.astype(jnp.float32) * attended.astype(jnp.float32), axis=-1)
    row_inner = row_inner.transpose(2, 0, 1)[..., None]
    grad_score = (weights * (grad_weight - row_inner)).astype(jnp.bfloat16)
    grad_query = jnp.einsum(
        "haim,hamd->aihd", grad_score, key_rows, preferred_element_type=jnp.float32
    )
    grad_query = (grad_query * score_scale).astype(jnp.bfloat16)
    grad_key_rows = (
        jnp.einsum("haim,aihd->hamd", grad_score, query_blocks, preferred_element_type=jnp.float32)
        * score_scale
    )
    grad_value_rows = jnp.einsum(
        "haim,aihd->hamd", weights_low, grad_blocks, preferred_element_type=jnp.float32
    )
    grad_key = scatter_blocks(grad_key_rows, layout, block_rows).astype(jnp.bfloat16)
    grad_value = scatter_blocks(grad_value_rows, layout, block_rows).astype(jnp.bfloat16)
    return (grad_query, grad_key, grad_value)


def local(queries, key_states, value_states, upstream, layout, segments):
    section_rows, tok_dev, feature_width = queries.shape
    head_dim = feature_width // HEADS

    def split_heads(field):
        return field.reshape(section_rows, tok_dev, HEADS, head_dim)

    arrived = passed_along(upstream, "section", -1)
    query_heads, key_heads, value_heads, grad_heads = (
        lax.all_to_all(split_heads(queries), "ctx", split_axis=2, concat_axis=1, tiled=True),
        lax.all_to_all(split_heads(key_states), "ctx", split_axis=2, concat_axis=1, tiled=True),
        lax.all_to_all(split_heads(value_states), "ctx", split_axis=2, concat_axis=1, tiled=True),
        lax.all_to_all(split_heads(arrived), "ctx", split_axis=2, concat_axis=1, tiled=True),
    )
    all_tokens = query_heads.shape[1]
    local_heads = query_heads.shape[2]
    block_count = all_tokens // BLK

    def to_blocks(field):
        return field[0].reshape(block_count, BLK, local_heads, head_dim)

    def to_rows(field):
        return field.reshape(1, all_tokens, local_heads, head_dim)

    query_blocks = to_blocks(query_heads)
    grad_blocks = to_blocks(grad_heads)
    plan = layout[0]
    documents = segments[0]
    attended, weights, weights_low, key_rows, value_rows = forward_part(
        query_blocks, to_blocks(key_heads), to_blocks(value_heads), plan, documents
    )
    grad_query, grad_key, grad_value = backward_part(
        query_blocks, grad_blocks, attended, weights, weights_low, key_rows, value_rows, plan
    )
    attended_back, query_back, key_back, value_back = (
        lax.all_to_all(to_rows(attended), "ctx", split_axis=1, concat_axis=2, tiled=True),
        lax.all_to_all(to_rows(grad_query), "ctx", split_axis=1, concat_axis=2, tiled=True),
        lax.all_to_all(to_rows(grad_key), "ctx", split_axis=1, concat_axis=2, tiled=True),
        lax.all_to_all(to_rows(grad_value), "ctx", split_axis=1, concat_axis=2, tiled=True),
    )

    def merge_heads(field):
        return field.reshape(section_rows, tok_dev, feature_width)

    return (
        merge_heads(attended_back),
        merge_heads(query_back),
        merge_heads(key_back),
        merge_heads(value_back),
    )


def solution(mesh):
    placed = (
        P("section", "ctx", None),
        P("section", "ctx", None),
        P("section", "ctx", None),
        P("section", "ctx", None),
        P("section", "ctx", None, None),
        P("section", None),
    )
    return jax.shard_map(
        local,
        mesh=mesh,
        in_specs=placed,
        out_specs=(
            P("section", "ctx", None),
            P("section", "ctx", None),
            P("section", "ctx", None),
            P("section", "ctx", None),
        ),
        check_vma=False,
    )
```

profile of v0, /device:TPU:0, one launch (start us, length us, event | category | flops | bytes accessed | tf_op | source)
XLA Modules:
  0.0 163.3 jit_solution(9700773874777066107)
XLA Ops:
  3.1 6.5 %all-to-all-start.1 = ((bf16[1,128,16,128]{3,1,0,2:T(8,128)(2,1)}), bf16[1,128,16,128]{3,1,0,2:T(8,128)(2,1)S(1)}, u32[]{:S(2)}, u32[]{:S(2)}) async-start(bf16[1,128,16,128]{3,1,0,2:T(8,128)(2,1)} %copy.114), calls=%async_computation.1 | async-start | bytes 1048576 | tf_op jit(solution)/shard_map/all_to_all | solution.py:115
  10.5 14.4 %all-to-all-done.1 = bf16[1,128,16,128]{3,1,0,2:T(8,128)(2,1)S(1)} async-done(((bf16[1,128,16,128]{3,1,0,2:T(8,128)(2,1)}), bf16[1,128,16,128]{3,1,0,2:T(8,128)(2,1)S(1)}, u32[]{:S(2)}, u32[]{:S(2)}) %all-to-all-start.1) | async-done | bytes 524320 | tf_op jit(solution)/shard_map/all_to_all | solution.py:115
  24.9 3.5 %all-to-all-start.2 = ((bf16[1,128,16,128]{1,3,0,2:T(8,128)(2,1)}), bf16[1,128,16,128]{1,3,0,2:T(8,128)(2,1)S(1)}, u32[]{:S(2)}, u32[]{:S(2)}) async-start(bf16[1,128,16,128]{1,3,0,2:T(8,128)(2,1)} %bitcast.18), calls=%async_computation.2 | async-start | bytes 1048576 | tf_op jit(solution)/shard_map/all_to_all | solution.py:114
  28.7 2.5 %collective-permute-start = (bf16[1,128,2048]{1,2,0:T(8,128)(2,1)S(1)}, bf16[1,128,2048]{1,2,0:T(8,128)(2,1)S(1)}, u32[]{:S(2)}, u32[]{:S(2)}) collective-permute-start(bf16[1,128,2048]{1,2,0:T(8,128)(2,1)S(1)} %copy.125), channel_id=1, source_target_pairs={{0,24},{8,0},{16,8},{24,16},{1,25},{9,1},{17,9},{25,17},{2,26},{10... | collective-permute-start | bytes 1572872 | tf_op jit(solution)/shard_map/ppermute | solution.py:15
  34.9 8.8 %all-to-all-done.2 = bf16[1,128,16,128]{1,3,0,2:T(8,128)(2,1)S(1)} async-done(((bf16[1,128,16,128]{1,3,0,2:T(8,128)(2,1)}), bf16[1,128,16,128]{1,3,0,2:T(8,128)(2,1)S(1)}, u32[]{:S(2)}, u32[]{:S(2)}) %all-to-all-start.2) | async-done | bytes 524320 | tf_op jit(solution)/shard_map/all_to_all | solution.py:114
  43.7 3.5 %all-to-all-start = ((bf16[1,128,16,128]{3,1,0,2:T(8,128)(2,1)}), bf16[1,128,16,128]{3,1,0,2:T(8,128)(2,1)S(1)}, u32[]{:S(2)}, u32[]{:S(2)}) async-start(bf16[1,128,16,128]{3,1,0,2:T(8,128)(2,1)} %copy.109), calls=%async_computation | async-start | bytes 1048576 | tf_op jit(solution)/shard_map/all_to_all | solution.py:116
  50.4 12.0 %all-to-all-done = bf16[1,128,16,128]{3,1,0,2:T(8,128)(2,1)S(1)} async-done(((bf16[1,128,16,128]{3,1,0,2:T(8,128)(2,1)}), bf16[1,128,16,128]{3,1,0,2:T(8,128)(2,1)S(1)}, u32[]{:S(2)}, u32[]{:S(2)}) %all-to-all-start) | async-done | bytes 524320 | tf_op jit(solution)/shard_map/all_to_all | solution.py:116
  62.5 4.1 %all-to-all-start.4 = ((bf16[1,128,16,128]{3,1,0,2:T(8,128)(2,1)}), bf16[1,128,16,128]{3,1,0,2:T(8,128)(2,1)}, u32[]{:S(2)}, u32[]{:S(2)}) async-start(bf16[1,128,16,128]{3,1,0,2:T(8,128)(2,1)} %copy.126), calls=%async_computation.4 | async-start | bytes 1048576 | tf_op jit(solution)/shard_map/all_to_all | solution.py:117
  66.6 2.2 %gather_fusion = bf16[64,128,128]{2,1,0:T(8,128)(2,1)} fusion(bf16[8,128,2,128]{3,1,2,0:T(8,128)(2,1)S(1)} %bitcast.161, s32[64]{0:T(128)S(1)} %reshape.182), kind=kCustom, calls=%fused_computation | custom fusion | bytes 4194816 | tf_op jit(solution)/shard_map/gather | solution.py:20
  68.9 6.0 %fusion.65 = (f32[2,8,128]{2,1,0:T(8,128)S(1)}, f32[2,8,128,512]{2,3,1,0:T(8,128)}) fusion(pred[128,512]{0,1:T(8,128)(4,1)S(1)} %bitcast.184, pred[2,8,512]{2,1,0:T(8,128)(4,1)S(1)} %get-tuple-element.30, pred[2,8,512]{2,1,0:T(8,128)(4,1)S(1)} %get-tuple-element.31, pred[2,8,512]{2,1,0:T(8,128)(4,1)S(1)} %broadcast_bitcast_fusion.2, ...), kind=kOutput, calls=%fused_computation.71 | convolution fusion | flops 275776000 | bytes 6914048 | tf_op jit(solution)/shard_map/sub | solution.py:69
  74.9 2.7 %fusion.15 = bf16[2,8,128,512]{2,3,1,0:T(8,128)(2,1)S(1)} fusion(f32[2,8,128,512]{2,3,1,0:T(8,128)} %get-tuple-element.27, f32[2,8,128]{2,1,0:T(8,128)S(1)} %get-tuple-element.26), kind=kLoop, calls=%fused_computation.26 | loop fusion | flops 2097152 | bytes 6299648 | tf_op jit(solution)/shard_map/convert_element_type | solution.py:71
  77.6 4.4 %all-to-all-done.4 = bf16[1,128,16,128]{3,1,0,2:T(8,128)(2,1)} async-done(((bf16[1,128,16,128]{3,1,0,2:T(8,128)(2,1)}), bf16[1,128,16,128]{3,1,0,2:T(8,128)(2,1)}, u32[]{:S(2)}, u32[]{:S(2)}) %all-to-all-start.4) | async-done | bytes 524320 | tf_op jit(solution)/shard_map/all_to_all | solution.py:117
  82.0 2.6 %multiply_reduce_fusion = (f32[8,128,2]{1,2,0:T(2,128)S(1)}, bf16[8,128,2,128]{3,1,2,0:T(8,128)(2,1)S(1)}) fusion(bf16[8,128,2,128]{3,1,2,0:T(8,128)(2,1)} %bitcast.31, bf16[2,8,128,512]{2,3,1,0:T(8,128)(2,1)S(1)} %fusion.15, bf16[2,8,512,128]{3,2,1,0:T(8,128)(2,1)} %bitcast.168), kind=kOutput, calls=%fused_computation.46 | convolution fusion | flops 269744128 | bytes 5251072 | tf_op jit(solution)/shard_map/haim,hamd->aihd/dot_general | solution.py:72
  86.0 3.5 %all-to-all-start.3 = ((bf16[1,1024,2,128]{3,2,0,1:T(2,128)(2,1)}), bf16[1,1024,2,128]{3,2,0,1:T(2,128)(2,1)S(1)}, u32[]{:S(2)}, u32[]{:S(2)}) async-start(bf16[1,1024,2,128]{3,2,0,1:T(2,128)(2,1)} %copy.122), calls=%async_computation.3 | async-start | bytes 1048576 | tf_op jit(solution)/shard_map/all_to_all | solution.py:140
  89.5 3.9 %fusion.1 = bf16[2,8,128,512]{2,3,1,0:T(8,128)(2,1)S(1)} fusion(bf16[2,8,512,128]{3,2,1,0:T(8,128)(2,1)} %bitcast.169, f32[2,8,128]{2,1,0:T(8,128)S(1)} %copy.128, f32[2,8,128,512]{2,3,1,0:T(8,128)} %get-tuple-element.27, f32[2,8,128]{2,1,0:T(8,128)S(1)} %get-tuple-element.26, bf16[8,128,2,128]{3,1,2,0:T(8,128)(2,1)} %bitcast.31), kind=kOutput, calls=%fused_computation.8 | convolution fusion | flops 272629760 | bytes 8929280 | tf_op jit(solution)/shard_map/aihd,hamd->haim/dot_general | solution.py:83
  96.1 8.6 %all-to-all-done.3 = bf16[1,1024,2,128]{3,2,0,1:T(2,128)(2,1)S(1)} async-done(((bf16[1,1024,2,128]{3,2,0,1:T(2,128)(2,1)}), bf16[1,1024,2,128]{3,2,0,1:T(2,128)(2,1)S(1)}, u32[]{:S(2)}, u32[]{:S(2)}) %all-to-all-start.3) | async-done | bytes 524320 | tf_op jit(solution)/shard_map/all_to_all | solution.py:140
  104.8 4.2 %all-to-all-start.5 = ((bf16[1,1024,2,128]{3,2,0,1:T(2,128)(2,1)}), bf16[1,1024,2,128]{3,2,0,1:T(2,128)(2,1)}, u32[]{:S(2)}, u32[]{:S(2)}) async-start(bf16[1,1024,2,128]{3,2,0,1:T(2,128)(2,1)} %copy.132), calls=%async_computation.5 | async-start | bytes 1048576 | tf_op jit(solution)/shard_map/all_to_all | solution.py:141
  108.9 2.3 %convolution_multiply_fusion = f32[2,8,512,128]{3,2,1,0:T(8,128)S(1)} fusion(bf16[2,8,128,512]{2,3,1,0:T(8,128)(2,1)} %copy-done.5, bf16[1,128,8,2,128]{4,1,2,3,0:T(8,128)(2,1)S(1)} %copy-done.9), kind=kOutput, calls=%fused_computation.12 | convolution fusion | flops 269484032 | bytes 6815744 | tf_op jit(solution)/shard_map/haim,aihd->hamd/dot_general | solution.py:94
  115.6 2.6 %scatter_fusion = f32[16,128,128]{2,1,0:T(8,128)S(1)} fusion(f32[16,128,128]{2,1,0:T(8,128)S(1)} %broadcast.72.clone, s32[16]{0:T(128)S(1)} %add_bitcast_fusion, f32[16,128,128]{2,1,0:T(8,128)} %bitcast.165), kind=kCustom, calls=%fused_computation.4 | custom fusion | flops 262144 | bytes 3145792 | tf_op jit(solution)/shard_map/scatter-add | solution.py:49
  121.8 2.5 %all-to-all-done.5 = bf16[1,1024,2,128]{3,2,0,1:T(2,128)(2,1)} async-done(((bf16[1,1024,2,128]{3,2,0,1:T(2,128)(2,1)}), bf16[1,1024,2,128]{3,2,0,1:T(2,128)(2,1)}, u32[]{:S(2)}, u32[]{:S(2)}) %all-to-all-start.5) | async-done | bytes 524320 | tf_op jit(solution)/shard_map/all_to_all | solution.py:141
  124.3 3.7 %all-to-all-start.6 = ((bf16[1,1024,2,128]{3,2,0,1:T(2,128)(2,1)}), bf16[1,1024,2,128]{3,2,0,1:T(2,128)(2,1)S(1)}, u32[]{:S(2)}, u32[]{:S(2)}) async-start(bf16[1,1024,2,128]{3,2,0,1:T(2,128)(2,1)} %bitcast.50), calls=%async_computation.6 | async-start | bytes 1048576 | tf_op jit(solution)/shard_map/all_to_all | solution.py:142
  139.2 3.9 %all-to-all-done.6 = bf16[1,1024,2,128]{3,2,0,1:T(2,128)(2,1)S(1)} async-done(((bf16[1,1024,2,128]{3,2,0,1:T(2,128)(2,1)}), bf16[1,1024,2,128]{3,2,0,1:T(2,128)(2,1)S(1)}, u32[]{:S(2)}, u32[]{:S(2)}) %all-to-all-start.6) | async-done | bytes 524320 | tf_op jit(solution)/shard_map/all_to_all | solution.py:142
  143.1 3.5 %all-to-all-start.7 = ((bf16[1,1024,2,128]{3,2,0,1:T(2,128)(2,1)}), bf16[1,1024,2,128]{3,2,0,1:T(2,128)(2,1)S(1)}, u32[]{:S(2)}, u32[]{:S(2)}) async-start(bf16[1,1024,2,128]{3,2,0,1:T(2,128)(2,1)} %bitcast.61), calls=%async_computation.7 | async-start | bytes 1048576 | tf_op jit(solution)/shard_map/all_to_all | solution.py:143
  151.8 10.0 %all-to-all-done.7 = bf16[1,1024,2,128]{3,2,0,1:T(2,128)(2,1)S(1)} async-done(((bf16[1,1024,2,128]{3,2,0,1:T(2,128)(2,1)}), bf16[1,1024,2,128]{3,2,0,1:T(2,128)(2,1)S(1)}, u32[]{:S(2)}, u32[]{:S(2)}) %all-to-all-start.7) | async-done | bytes 524320 | tf_op jit(solution)/shard_map/all_to_all | solution.py:143
  (98 shorter events, 40.3 us)
Async XLA Ops:
  0.6 30.8 %copy-start = (s32[1,8]{1,0:T(1,128)S(1)}, s32[1,8]{1,0:T(1,128)}, u32[]{:S(2)}) copy-start(s32[1,8]{1,0:T(1,128)} %param.11) | copy-start | bytes 100
  0.6 8.9 %copy-start.10 = (bf16[1,128,2048]{2,1,0:T(8,128)(2,1)S(1)}, bf16[1,128,2048]{2,1,0:T(8,128)(2,1)}, u32[]{:S(2)}) copy-start(bf16[1,128,2048]{2,1,0:T(8,128)(2,1)} %param.6) | copy-start | bytes 1572868
  2.0 26.4 %copy-start.11 = (bf16[1,128,2048]{2,1,0:T(8,128)(2,1)S(1)}, bf16[1,128,2048]{2,1,0:T(8,128)(2,1)}, u32[]{:S(2)}) copy-start(bf16[1,128,2048]{2,1,0:T(8,128)(2,1)} %param.9) | copy-start | bytes 1572868
  3.1 28.1 %copy-start.13 = (s32[1,2,8,4]{2,3,1,0:T(4,128)S(1)}, s32[1,2,8,4]{2,3,1,0:T(4,128)}, u32[]{:S(2)}) copy-start(s32[1,2,8,4]{2,3,1,0:T(4,128)} %param.10) | copy-start | bytes 772
  3.1 21.8 %all-to-all-start.1 = ((bf16[1,128,16,128]{3,1,0,2:T(8,128)(2,1)}), bf16[1,128,16,128]{3,1,0,2:T(8,128)(2,1)S(1)}, u32[]{:S(2)}, u32[]{:S(2)}) async-start(bf16[1,128,16,128]{3,1,0,2:T(8,128)(2,1)} %copy.114), calls=%async_computation.1 | async-start | bytes 1048576 | tf_op jit(solution)/shard_map/all_to_all | solution.py:115
  24.9 18.8 %all-to-all-start.2 = ((bf16[1,128,16,128]{1,3,0,2:T(8,128)(2,1)}), bf16[1,128,16,128]{1,3,0,2:T(8,128)(2,1)S(1)}, u32[]{:S(2)}, u32[]{:S(2)}) async-start(bf16[1,128,16,128]{1,3,0,2:T(8,128)(2,1)} %bitcast.18), calls=%async_computation.2 | async-start | bytes 1048576 | tf_op jit(solution)/shard_map/all_to_all | solution.py:114
  28.7 18.7 %collective-permute-start = (bf16[1,128,2048]{1,2,0:T(8,128)(2,1)S(1)}, bf16[1,128,2048]{1,2,0:T(8,128)(2,1)S(1)}, u32[]{:S(2)}, u32[]{:S(2)}) collective-permute-start(bf16[1,128,2048]{1,2,0:T(8,128)(2,1)S(1)} %copy.125), channel_id=1, source_target_pairs={{0,24},{8,0},{16,8},{24,16},{1,25},{9,1},{17,9},{25,17},{2,26},{10... | collective-permute-start | bytes 1572872 | tf_op jit(solution)/shard_map/ppermute | solution.py:15
  31.4 1.9 %copy-start.12 = (bf16[1,128,2048]{2,1,0:T(8,128)(2,1)S(1)}, bf16[1,128,2048]{2,1,0:T(8,128)(2,1)}, u32[]{:S(2)}) copy-start(bf16[1,128,2048]{2,1,0:T(8,128)(2,1)} %param.8) | copy-start | bytes 1572868
  43.7 18.8 %all-to-all-start = ((bf16[1,128,16,128]{3,1,0,2:T(8,128)(2,1)}), bf16[1,128,16,128]{3,1,0,2:T(8,128)(2,1)S(1)}, u32[]{:S(2)}, u32[]{:S(2)}) async-start(bf16[1,128,16,128]{3,1,0,2:T(8,128)(2,1)} %copy.109), calls=%async_computation | async-start | bytes 1048576 | tf_op jit(solution)/shard_map/all_to_all | solution.py:116
  50.4 18.4 %copy-start.3 = (bf16[64,128,128]{2,1,0:T(8,128)(2,1)}, bf16[64,128,128]{2,1,0:T(8,128)(2,1)S(1)}, u32[]{:S(2)}) copy-start(bf16[64,128,128]{2,1,0:T(8,128)(2,1)S(1)} %gather_fusion.3) | copy-start | bytes 6291460
  62.5 19.5 %all-to-all-start.4 = ((bf16[1,128,16,128]{3,1,0,2:T(8,128)(2,1)}), bf16[1,128,16,128]{3,1,0,2:T(8,128)(2,1)}, u32[]{:S(2)}, u32[]{:S(2)}) async-start(bf16[1,128,16,128]{3,1,0,2:T(8,128)(2,1)} %copy.126), calls=%async_computation.4 | async-start | bytes 1048576 | tf_op jit(solution)/shard_map/all_to_all | solution.py:117
  66.6 2.2 %copy-start.8 = (bf16[1,128,8,2,128]{4,1,2,3,0:T(8,128)(2,1)S(1)}, bf16[1,128,8,2,128]{4,1,2,3,0:T(8,128)(2,1)}, u32[]{:S(2)}) copy-start(bf16[1,128,8,2,128]{4,1,2,3,0:T(8,128)(2,1)} %copy.118) | copy-start | bytes 1572868
  86.0 18.8 %all-to-all-start.3 = ((bf16[1,1024,2,128]{3,2,0,1:T(2,128)(2,1)}), bf16[1,1024,2,128]{3,2,0,1:T(2,128)(2,1)S(1)}, u32[]{:S(2)}, u32[]{:S(2)}) async-start(bf16[1,1024,2,128]{3,2,0,1:T(2,128)(2,1)} %copy.122), calls=%async_computation.3 | async-start | bytes 1048576 | tf_op jit(solution)/shard_map/all_to_all | solution.py:140
  89.5 3.9 %copy-start.4 = (bf16[64,128,128]{2,1,0:T(8,128)(2,1)S(1)}, bf16[64,128,128]{2,1,0:T(8,128)(2,1)}, u32[]{:S(2)}) copy-start(bf16[64,128,128]{2,1,0:T(8,128)(2,1)} %copy-done.3) | copy-start | bytes 6291460
  93.4 1.3 copy-start.5
  94.7 14.2 %copy-start.9 = (bf16[1,128,8,2,128]{4,1,2,3,0:T(8,128)(2,1)S(1)}, bf16[1,128,8,2,128]{4,1,2,3,0:T(8,128)(2,1)}, u32[]{:S(2)}) copy-start(bf16[1,128,8,2,128]{4,1,2,3,0:T(8,128)(2,1)} %copy.118) | copy-start | bytes 1572868
  104.8 6.5 %copy-start.6 = (bf16[1,1024,2,128]{3,2,0,1:T(2,128)(2,1)}, bf16[1,1024,2,128]{3,2,0,1:T(2,128)(2,1)S(1)}, u32[]{:S(2)}) copy-start(bf16[1,1024,2,128]{3,2,0,1:T(2,128)(2,1)S(1)} %all-to-all-done.3) | copy-start | bytes 1572868
  104.8 19.5 %all-to-all-start.5 = ((bf16[1,1024,2,128]{3,2,0,1:T(2,128)(2,1)}), bf16[1,1024,2,128]{3,2,0,1:T(2,128)(2,1)}, u32[]{:S(2)}, u32[]{:S(2)}) async-start(bf16[1,1024,2,128]{3,2,0,1:T(2,128)(2,1)} %copy.132), calls=%async_computation.5 | async-start | bytes 1048576 | tf_op jit(solution)/shard_map/all_to_all | solution.py:141
  111.2 2.3 %copy-start.2 = (f32[2,8,512,128]{3,2,1,0:T(8,128)}, f32[2,8,512,128]{3,2,1,0:T(8,128)S(1)}, u32[]{:S(2)}) copy-start(f32[2,8,512,128]{3,2,1,0:T(8,128)S(1)} %convolution_multiply_fusion) | copy-start | bytes 12582916
  124.3 18.8 %all-to-all-start.6 = ((bf16[1,1024,2,128]{3,2,0,1:T(2,128)(2,1)}), bf16[1,1024,2,128]{3,2,0,1:T(2,128)(2,1)S(1)}, u32[]{:S(2)}, u32[]{:S(2)}) async-start(bf16[1,1024,2,128]{3,2,0,1:T(2,128)(2,1)} %bitcast.50), calls=%async_computation.6 | async-start | bytes 1048576 | tf_op jit(solution)/shard_map/all_to_all | solution.py:142
  129.7 1.9 %copy-start.1 = (f32[2,8,512,128]{3,2,1,0:T(8,128)}, f32[2,8,512,128]{3,2,1,0:T(8,128)S(1)}, u32[]{:S(2)}) copy-start(f32[2,8,512,128]{3,2,1,0:T(8,128)S(1)} %fusion.54) | copy-start | bytes 12582916
  137.8 8.8 %copy-start.7 = (bf16[1,1024,2,128]{3,2,0,1:T(2,128)(2,1)S(1)}, bf16[1,1024,2,128]{3,2,0,1:T(2,128)(2,1)}, u32[]{:S(2)}) copy-start(bf16[1,1024,2,128]{3,2,0,1:T(2,128)(2,1)} %copy-done.6) | copy-start | bytes 1572868
  143.1 18.8 %all-to-all-start.7 = ((bf16[1,1024,2,128]{3,2,0,1:T(2,128)(2,1)}), bf16[1,1024,2,128]{3,2,0,1:T(2,128)(2,1)S(1)}, u32[]{:S(2)}, u32[]{:S(2)}) async-start(bf16[1,1024,2,128]{3,2,0,1:T(2,128)(2,1)} %bitcast.61), calls=%async_computation.7 | async-start | bytes 1048576 | tf_op jit(solution)/shard_map/all_to_all | solution.py:143
where the time goes:
time: 164 us; the launch traced here: 163 us
  waiting for transfers between devices  64.7 us (39%)
  starting transfers between devices  34.9 us (21%)
  local copies, waits for them, and re-layouts  34 us (21%)
  matrix products  17.3 us (11%)
  other arithmetic  11.2 us (7%)
    all_to_all x1, waiting for transfers between devices, local(): lax.all_to_all(split_heads(key_states), 'ctx', split_axis=2, concat_axis=...  14.4 us
    all_to_all x1, waiting for transfers between devices, local(): lax.all_to_all(split_heads(value_states), 'ctx', split_axis=2, concat_axi...  12 us
    unnamed x36, local copies, waits for them, and re-layouts  10.1 us
    all_to_all x1, waiting for transfers between devices, local(): lax.all_to_all(to_rows(grad_value), 'ctx', split_axis=1, concat_axis=2, t...  10 us
    all_to_all x1, waiting for transfers between devices, local(): lax.all_to_all(split_heads(queries), 'ctx', split_axis=2, concat_axis=1,...  8.77 us
    all_to_all x1, waiting for transfers between devices, local(): lax.all_to_all(to_rows(attended), 'ctx', split_axis=1, concat_axis=2, til...  8.63 us
    all_to_all x1, starting transfers between devices, local(): lax.all_to_all(split_heads(key_states), 'ctx', split_axis=2, concat_axis=...  6.46 us
    sub x1, matrix products, forward_part(): raised = jnp.exp(scores - row_max)  5.99 us
  transfers between devices with their start and end apart: 9, of which 8 were waited for; matrix products, arithmetic and copies ran while one was open for 32% of the time, Pallas kernels for 0%

commit v1 on v0

v1 whole, which is shorter than its diff:
```python
import functools
import math

import jax
import jax.numpy as jnp
from jax import lax
from jax.experimental import pallas as pl
from jax.experimental.pallas import tpu as pltpu
from jax.sharding import PartitionSpec as P

HEADS = 16
BLK = 128
CORES = 2
LEAD = 2
HIDDEN = -1e30
MESH = pl.DeviceIdType.MESH


def dot(left, right, left_dim, right_dim):
    return lax.dot_general(
        left, right, (((left_dim,), (right_dim,)), ((), ())), preferred_element_type=jnp.float32
    )


def kernel(
    sections,
    count,
    head_dim,
    seg_ref,
    far_ref,
    q_ref,
    k_ref,
    v_ref,
    u_ref,
    o_ref,
    dq_ref,
    dk_ref,
    dv_ref,
    kvw,
    qb,
    gb,
    fart,
    bias,
    acc,
    snd,
    rcv,
    st,
    up_send,
    up_recv,
    fw_send,
    fw_recv,
    dn_send,
    dn_recv,
    xc_send,
    xc_recv,
    u_send,
    u_recv,
    fa_send,
    fa_recv,
    ou_send,
    ou_recv,
):
    chips = count // CORES
    heads = HEADS // CORES
    reach = count // 2 - 1
    hops = (reach + 1) // 2
    scale = 1.0 / math.sqrt(head_dim)
    sec = lax.axis_index("section")
    me = lax.axis_index("ctx")
    chip = me // CORES
    core = me % CORES
    other = 1 - core
    sibling = chip * CORES + other
    before_sec = (sec + sections - 1) % sections
    after_sec = (sec + 1) % sections
    inputs = (q_ref, k_ref, v_ref)
    results = (o_ref, dq_ref, dk_ref, dv_ref)

    def cols(h):
        return pl.ds(pl.multiple_of(h * head_dim, head_dim), head_dim)

    def half(side):
        return pl.ds(pl.multiple_of(side * (heads * head_dim), heads * head_dim), heads * head_dim)

    def rows(block, n=1):
        if isinstance(block, int):
            return pl.ds(block * BLK, n * BLK)
        return pl.ds(pl.multiple_of(block * BLK, BLK), n * BLK)

    def hop_rows(hop):
        first = reach - 2 * hop
        return rows(0, 1) if first < 0 else rows(first, 2)

    def remote(src, dst, send, recv, section, ctx):
        return pltpu.make_async_remote_copy(
            src_ref=src,
            dst_ref=dst,
            send_sem=send,
            recv_sem=recv,
            device_id=(section, ctx),
            device_id_type=MESH,
        )

    def up(h, to_core, kv, source):
        return remote(
            inputs[1 + kv].at[0, :, cols(to_core * heads + h)],
            kvw.at[kv, rows(reach - 2 + source), cols(h)],
            up_send.at[to_core, kv, h],
            up_recv.at[source, kv, h],
            sec,
            me - core + CORES + to_core,
        )

    def forward(h, hop):
        full = reach - 2 * hop >= 0
        source = rows(reach - 2 * hop + 2, 2) if full else rows(reach - 2 * hop + 3, 1)
        return remote(
            kvw.at[:, source, cols(h)],
            kvw.at[:, hop_rows(hop), cols(h)],
            fw_send.at[hop - 2, h],
            fw_recv.at[hop - 2, h],
            sec,
            me + CORES,
        )

    def down(h, hop):
        return remote(
            snd.at[:, hop_rows(hop), cols(h)],
            rcv.at[:, hop_rows(hop), cols(h)],
            dn_send.at[hop - 1, h],
            dn_recv.at[hop - 1, h],
            sec,
            me - CORES,
        )

    def swap(x, block):
        dst = qb.at[rows(block), :] if x == 0 else kvw.at[x - 1, rows(reach + block), :]
        return remote(
            inputs[x].at[0, :, half(other)], dst, xc_send.at[x], xc_recv.at[x], sec, sibling
        )

    def relay(h, to_core, source):
        return remote(
            u_ref.at[0, :, cols(to_core * heads + h)],
            gb.at[rows(source), cols(h)],
            u_send.at[to_core, h],
            u_recv.at[source, h],
            before_sec,
            me - core + to_core,
        )

    held = HEADS // count
    side = me // chips
    place = me % chips

    def spread(to_chip, slot):
        return remote(
            far_ref,
            fart.at[pl.ds(slot * held, held)],
            fa_send.at[to_chip],
            fa_recv.at[slot],
            sec,
            to_chip * CORES + side,
        )

    def give(h, x):
        return remote(
            st.at[x, rows(other), cols(h)],
            results[x].at[0, :, cols(core * heads + h)],
            ou_send.at[x, h],
            ou_recv.at[x, h],
            sec,
            sibling,
        )

    def take(h, x):
        return remote(
            st.at[x, rows(core), cols(h)],
            results[x].at[0, :, cols(other * heads + h)],
            ou_send.at[x, h],
            ou_recv.at[x, h],
            sec,
            sibling,
        )

    barrier = pltpu.get_barrier_semaphore()
    for step in range(1, count):
        pl.semaphore_signal(
            barrier, inc=1, device_id=(sec, (me + step) % count), device_id_type=MESH
        )
    for section in (before_sec, after_sec):
        for to_core in range(CORES):
            pl.semaphore_signal(
                barrier, inc=1, device_id=(section, me - core + to_core), device_id_type=MESH
            )

    for hop in range(1, hops + 1):

        @pl.when(chip < hop)
        def _():
            first = max(reach - 2 * hop, 0)
            height = (1 if reach - 2 * hop < 0 else 2) * BLK
            kvw[:, pl.ds(first * BLK, height), :] = jnp.zeros(
                (2, height, heads * head_dim), kvw.dtype
            )

    qb[rows(core), :] = q_ref[0, :, half(core)]
    kvw[0, rows(reach + core), :] = k_ref[0, :, half(core)]
    kvw[1, rows(reach + core), :] = v_ref[0, :, half(core)]

    pl.semaphore_wait(barrier, count - 1 + 2 * CORES)

    def send_up(h):
        @pl.when(chip < chips - 1)
        def _():
            for kv in range(2):
                for to_core in range(CORES):
                    up(h, to_core, kv, core).start()

    def send_relay(h):
        for to_core in range(CORES):
            relay(h, to_core, core).start()

    for h in range(LEAD):
        send_up(h)
    for step in range(chips):

        @pl.when(jnp.logical_not(step * CORES + side == me))
        def _():
            spread(step, place).start()

    @pl.when(side == core)
    def _():
        fart[pl.ds(place * held, held)] = far_ref[...]

    for x in range(3):
        swap(x, core).start()
    for h in range(LEAD + 1):
        send_relay(h)

    row_id = lax.broadcasted_iota(jnp.int32, (BLK, BLK), 0)
    col_id = lax.broadcasted_iota(jnp.int32, (BLK, BLK), 1)
    causal = jnp.where(col_id <= row_id, 0.0, HIDDEN).astype(jnp.float32)
    for qi in range(2):
        doc = seg_ref[0, chip * CORES + qi]
        for i in range(reach + 1):
            block = chip * CORES + qi - reach + i
            same = jnp.logical_and(block >= 0, seg_ref[0, jnp.maximum(block, 0)] == doc)
            shown = jnp.where(same, 0.0, HIDDEN).astype(jnp.float32)
            here = causal if i == reach else jnp.zeros((BLK, BLK), jnp.float32)
            bias[pl.ds(qi * BLK, BLK), pl.ds(i * BLK, BLK)] = here + shown

    for x in range(3):
        swap(x, other).wait_recv()
    for step in range(chips):

        @pl.when(jnp.logical_not(core * chips + step == me))
        def _():
            spread(0, step).wait_recv()

    def compute(h):
        part = cols(h)
        weights_of, score_of, q_of, g_of = [], [], [], []
        for qi in range(2):
            q = qb[pl.ds(qi * BLK, BLK), part]
            g = gb[pl.ds(qi * BLK, BLK), part]
            keys = kvw[0, pl.ds(qi * BLK, (reach + 1) * BLK), part]
            values = kvw[1, pl.ds(qi * BLK, (reach + 1) * BLK), part]
            block = chip * CORES + qi
            far = fart[h, pl.ds(block, 1), :]
            pieces = []
            for i in range(reach + 1):
                if reach - i >= 3:
                    pieces.append(
                        jnp.where(far == block - reach + i, 0.0, HIDDEN).astype(jnp.float32)
                    )
                else:
                    pieces.append(jnp.zeros((1, BLK), jnp.float32))
            scores = dot(q, keys, 1, 1) * scale + bias[pl.ds(qi * BLK, BLK), :]
            scores = scores + jnp.concatenate(pieces, axis=1)
            row_max = jnp.max(scores, axis=-1, keepdims=True)
            raised = jnp.exp(scores - row_max)
            weights = raised * (1.0 / jnp.sum(raised, axis=-1, keepdims=True))
            low = weights.astype(jnp.bfloat16)
            attended = dot(low, values, 1, 0).astype(jnp.bfloat16)
            st[0, pl.ds(qi * BLK, BLK), part] = attended
            inner = jnp.sum(
                g.astype(jnp.float32) * attended.astype(jnp.float32), axis=-1, keepdims=True
            )
            score = (weights * (dot(g, values, 1, 1) - inner)).astype(jnp.bfloat16)
            st[1, pl.ds(qi * BLK, BLK), part] = (dot(score, keys, 1, 0) * scale).astype(
                jnp.bfloat16
            )
            weights_of.append(low)
            score_of.append(score)
            q_of.append(q)
            g_of.append(g)
        for kv, (left, right, factor) in enumerate(
            ((score_of, q_of, scale), (weights_of, g_of, 1.0))
        ):
            acc[h, kv, pl.ds(0, BLK), :] = dot(left[0][:, :BLK], right[0], 0, 0) * factor
            acc[h, kv, pl.ds((reach + 1) * BLK, BLK), :] = (
                dot(left[1][:, reach * BLK :], right[1], 0, 0) * factor
            )
            both = jnp.concatenate([left[0][:, BLK:], left[1][:, : reach * BLK]], axis=0)
            acc[h, kv, pl.ds(BLK, reach * BLK), :] = (
                dot(both, jnp.concatenate(right, axis=0), 0, 0) * factor
            )

    def hand_out(h, x):
        give(h, x).start()
        results[x][0, :, cols(core * heads + h)] = st[x, rows(core), cols(h)]

    def send_down(h, hop):
        @pl.when(chip >= hop)
        def _():
            for kv in range(2):
                snd[kv, hop_rows(hop), cols(h)] = acc[h, kv, hop_rows(hop), :].astype(jnp.bfloat16)
            down(h, hop).start()

    def at(h, action):
        @pl.when(jnp.logical_and(h >= 0, h < heads))
        def _():
            action(h)

    def arrive(hop):
        def action(h):
            @pl.when(chip >= hop)
            def _():
                if hop == 1:
                    for source in range(CORES):
                        for kv in range(2):
                            up(h, 0, kv, source).wait_recv()
                else:
                    forward(h, hop).wait_recv()

            if hop < hops:

                @pl.when(jnp.logical_and(chip >= hop, chip < chips - 1))
                def _():
                    forward(h, hop + 1).start()

        return action

    def work(h):
        for source in range(CORES):
            relay(h, 0, source).wait_recv()
        compute(h)
        send_down(h, hops)
        for x in range(2):
            hand_out(h, x)

    def settle(hop):
        def action(h):
            target = max(reach - 2 * hop + 2, 0) if reach - 2 * hop >= 0 else 2
            if reach - 2 * hop < 0:
                target = reach - 2 * hop + 3
            height = BLK if reach - 2 * hop < 0 else 2 * BLK

            @pl.when(jnp.logical_and(chip < chips - 1, chip + 1 >= hop))
            def _():
                down(h, hop).wait_recv()
                for kv in range(2):
                    acc[h, kv, pl.ds(target * BLK, height), :] += rcv[
                        kv, hop_rows(hop), cols(h)
                    ].astype(jnp.float32)

            if hop > 1:
                send_down(h, hop - 1)
            else:
                for kv in range(2):
                    st[2 + kv, :, cols(h)] = acc[h, kv, pl.ds(reach * BLK, 2 * BLK), :].astype(
                        jnp.bfloat16
                    )
                    hand_out(h, 2 + kv)

        return action

    @pl.loop(0, heads + 2 * hops - 1)
    def _(i):
        @pl.when(i + LEAD < heads)
        def _():
            send_up(i + LEAD)

        @pl.when(i + LEAD + 1 < heads)
        def _():
            send_relay(i + LEAD + 1)

        for hop in range(1, hops + 1):
            at(i - (hop - 1), arrive(hop))
        at(i - (hops - 1), work)
        for hop in range(hops, 0, -1):
            at(i - (hops - 1) - 1 - (hops - hop), settle(hop))

    for x in range(3):
        swap(x, core).wait_send()
    for step in range(chips):

        @pl.when(jnp.logical_not(step * CORES + side == me))
        def _():
            spread(step, place).wait_send()

    @pl.loop(0, heads)
    def _(h):
        @pl.when(chip < chips - 1)
        def _():
            for kv in range(2):
                for to_core in range(CORES):
                    up(h, to_core, kv, core).wait_send()

        for hop in range(2, hops + 1):

            @pl.when(jnp.logical_and(chip >= hop - 1, chip < chips - 1))
            def _():
                forward(h, hop).wait_send()

        for hop in range(1, hops + 1):

            @pl.when(chip >= hop)
            def _():
                down(h, hop).wait_send()

        for to_core in range(CORES):
            relay(h, to_core, core).wait_send()
        for x in range(4):
            give(h, x).wait_send()
            take(h, x).wait_recv()


def local(queries, key_states, value_states, upstream, layout, segments):
    sections = lax.axis_size("section")
    count = lax.axis_size("ctx")
    width = queries.shape[-1]
    head_dim = width // HEADS
    heads = HEADS // CORES
    held, blocks, _ = layout.shape[1:]
    chips = count // CORES
    reach = count // 2 - 1
    hops = (reach + 1) // 2
    plan = layout[0]
    distance = (jnp.arange(blocks, dtype=jnp.int32)[None, :, None] - plan + blocks) % blocks
    far = jnp.sum(jnp.where(distance >= 3, plan, 0), axis=-1)
    far = jnp.broadcast_to(far[:, :, None], (held, blocks, BLK)).astype(jnp.int32)
    vmem = pl.BlockSpec(memory_space=pltpu.VMEM)
    part = heads * head_dim
    dma = pltpu.SemaphoreType.DMA
    return tuple(
        pl.pallas_call(
            functools.partial(kernel, sections, count, head_dim),
            out_shape=[jax.ShapeDtypeStruct(queries.shape, jnp.bfloat16)] * 4,
            in_specs=[pl.BlockSpec(memory_space=pltpu.SMEM)] + [vmem] * 5,
            out_specs=[vmem] * 4,
            scratch_shapes=[
                pltpu.VMEM((2, (reach + 2) * BLK, part), jnp.bfloat16),
                pltpu.VMEM((2 * BLK, part), jnp.bfloat16),
                pltpu.VMEM((2 * BLK, part), jnp.bfloat16),
                pltpu.VMEM((heads, blocks, BLK), jnp.int32),
                pltpu.VMEM((2 * BLK, (reach + 1) * BLK), jnp.float32),
                pltpu.VMEM((heads, 2, (reach + 2) * BLK, head_dim), jnp.float32),
                pltpu.VMEM((2, reach * BLK, part), jnp.bfloat16),
                pltpu.VMEM((2, reach * BLK, part), jnp.bfloat16),
                pltpu.VMEM((4, 2 * BLK, part), jnp.bfloat16),
                dma((CORES, 2, heads)),
                dma((CORES, 2, heads)),
                dma((max(hops - 1, 1), heads)),
                dma((max(hops - 1, 1), heads)),
                dma((hops, heads)),
                dma((hops, heads)),
                dma((3,)),
                dma((3,)),
                dma((CORES, heads)),
                dma((CORES, heads)),
                dma((chips,)),
                dma((chips,)),
                dma((4, heads)),
                dma((4, heads)),
            ],
            compiler_params=pltpu.CompilerParams(
                collective_id=0, has_side_effects=True, vmem_limit_bytes=44 * 1024 * 1024
            ),
        )(segments, far, queries, key_states, value_states, upstream)
    )


def solution(mesh):
    field = P("section", "ctx", None)
    return jax.shard_map(
        local,
        mesh=mesh,
        in_specs=(field,) * 4 + (P("section", "ctx", None, None), P("section", None)),
        out_specs=(field,) * 4,
        check_vma=False,
    )
```

time: 164 us -> 71.3 us (0.43)
  waiting for transfers between devices: 64.7 us -> 0 us
  Pallas kernels: 0 us -> 61.6 us
  starting transfers between devices: 34.9 us -> 0 us
  local copies, waits for them, and re-layouts: 34 us -> 7.99 us
  matrix products: 17.3 us -> 0 us
  other arithmetic: 11.2 us -> 0.72 us
    all_to_all x8 -> x0, waiting for transfers between devices: 64.6 us -> none  [the longest x1 14.4 us: local(): lax.all_to_all(split_heads(key_states), 'ctx', split_axis=2, concat_axis=...]
    pallas_call x0 -> x1, Pallas kernels: none -> 61.6 us  [local(): pl.pallas_call(functools.partial(kernel, sections, count, head_dim), out_...]
    all_to_all x8 -> x0, starting transfers between devices: 32.4 us -> none  [the longest x1 6.46 us: local(): lax.all_to_all(split_heads(key_states), 'ctx', split_axis=2, concat_axis=...]
    dot_general x5 -> x0, matrix products: 11.3 us -> none  [the longest x1 3.88 us: backward_part(): jnp.einsum('aihd,hamd->haim', grad_blocks, value_rows, preferred_element_...]
    convert_element_type x3 -> x0, other arithmetic: 6.9 us -> none  [the longest x1 2.69 us: forward_part(): weights_low = weights.astype(jnp.bfloat16)]
    sub x1 -> x0, matrix products: 5.99 us -> none  [forward_part(): raised = jnp.exp(scores - row_max)]
    reshape x5 -> x0, local copies, waits for them, and re-layouts: 5.74 us -> none  [the longest x3 3.07 us: split_heads(): return field.reshape(section_rows, tok_dev, HEADS, head_dim)]
    gather x5 -> x0, local copies, waits for them, and re-layouts: 4.66 us -> none  [the longest x2 3.16 us: gather_blocks(): picked = blocks[layout, :, head_index, :]]
  transfers between devices with their start and end apart: 9 -> 0, of which waited for: 8 -> 0; matrix products, arithmetic and copies ran while one was open for 32% -> 0% of each run, Pallas kernels for 0% -> 0%
where the time goes in v1:
time: 71.3 us; the launch traced here: 71 us
  Pallas kernels  61.6 us (86%)
  local copies, waits for them, and re-layouts  7.99 us (11%)
  other arithmetic  0.72 us (1%)
    pallas_call x1, Pallas kernels, local(): pl.pallas_call(functools.partial(kernel, sections, count, head_dim), out_...  61.6 us
    unnamed x14, local copies, waits for them, and re-layouts  7.92 us

profile of v1, /device:TPU:0, one launch (start us, length us, event | category | flops | bytes accessed | tf_op | source)
XLA Modules:
  0.0 71.0 jit_solution(13913850703357849892)
XLA Ops:
  0.6 0.7 %fusion.3 = s32[2,8]{1,0:T(2,128)S(1)} fusion(s32[1,2,8,4]{2,3,1,0:T(4,128)} %param.10), kind=kLoop, calls=%fused_computation.8 | loop fusion | flops 1008 | bytes 320 | tf_op jit(solution)/shard_map/reduce_sum | solution.py:442
  1.3 0.0 copy-start.4
  1.4 0.1 broadcast_in_dim.4.far_ref
  1.4 0.6 copy-done.4
  2.0 0.0 copy-start
  2.0 1.0 %copy-done = bf16[1,128,2048]{2,1,0:T(8,128)(2,1)S(1)} copy-done((bf16[1,128,2048]{2,1,0:T(8,128)(2,1)S(1)}, bf16[1,128,2048]{2,1,0:T(8,128)(2,1)}, u32[]{:S(2)}) %copy-start) | copy-done | bytes 524312
  3.0 0.0 copy-start.1
  3.0 1.0 %copy-done.1 = bf16[1,128,2048]{2,1,0:T(8,128)(2,1)S(1)} copy-done((bf16[1,128,2048]{2,1,0:T(8,128)(2,1)S(1)}, bf16[1,128,2048]{2,1,0:T(8,128)(2,1)}, u32[]{:S(2)}) %copy-start.1) | copy-done | bytes 524312
  4.1 0.0 copy-start.2
  4.1 1.0 %copy-done.2 = bf16[1,128,2048]{2,1,0:T(8,128)(2,1)S(1)} copy-done((bf16[1,128,2048]{2,1,0:T(8,128)(2,1)S(1)}, bf16[1,128,2048]{2,1,0:T(8,128)(2,1)}, u32[]{:S(2)}) %copy-start.2) | copy-done | bytes 524312
  5.1 0.0 copy-start.3
  5.1 1.0 %copy-done.3 = bf16[1,128,2048]{2,1,0:T(8,128)(2,1)S(1)} copy-done((bf16[1,128,2048]{2,1,0:T(8,128)(2,1)S(1)}, bf16[1,128,2048]{2,1,0:T(8,128)(2,1)}, u32[]{:S(2)}) %copy-start.3) | copy-done | bytes 524312
  6.2 61.6 %shard_map.93 = (bf16[1,128,2048]{2,1,0:T(8,128)(2,1)S(1)}, bf16[1,128,2048]{2,1,0:T(8,128)(2,1)S(1)}, bf16[1,128,2048]{2,1,0:T(8,128)(2,1)S(1)}, bf16[1,128,2048]{2,1,0:T(8,128)(2,1)S(1)}) custom-call(s32[1,8]{1,0:T(1,128)S(1)} %copy-done.4, s32[2,8,128]{2,1,0:T(8,128)S(1)} %broadcast_in_dim.4.far_ref, bf16[1,128,2048]{2,1,0:T(8,128)(2,1)S(1)} %copy-done, ...), custom_call_target="tpu_custom_call" | custom-call | tf_op jit(solution)/shard_map/pallas_call | solution.py:448
  67.8 0.8 %copy.14 = bf16[1,128,2048]{2,1,0:T(8,128)(2,1)} copy(bf16[1,128,2048]{2,1,0:T(8,128)(2,1)S(1)} %get-tuple-element.8) | data formatting | bytes 1048576
  68.6 0.8 %copy.15 = bf16[1,128,2048]{2,1,0:T(8,128)(2,1)} copy(bf16[1,128,2048]{2,1,0:T(8,128)(2,1)S(1)} %get-tuple-element.9) | data formatting | bytes 1048576
  69.4 0.8 %copy.16 = bf16[1,128,2048]{2,1,0:T(8,128)(2,1)} copy(bf16[1,128,2048]{2,1,0:T(8,128)(2,1)S(1)} %get-tuple-element.10) | data formatting | bytes 1048576
  70.2 0.8 %copy.17 = bf16[1,128,2048]{2,1,0:T(8,128)(2,1)} copy(bf16[1,128,2048]{2,1,0:T(8,128)(2,1)S(1)} %get-tuple-element.11) | data formatting | bytes 1048576
Async XLA Ops:
  1.3 0.7 copy-start.4
  2.0 1.0 %copy-start = (bf16[1,128,2048]{2,1,0:T(8,128)(2,1)S(1)}, bf16[1,128,2048]{2,1,0:T(8,128)(2,1)}, u32[]{:S(2)}) copy-start(bf16[1,128,2048]{2,1,0:T(8,128)(2,1)} %q_ref.1) | copy-start | bytes 1572868
  3.0 1.0 %copy-start.1 = (bf16[1,128,2048]{2,1,0:T(8,128)(2,1)S(1)}, bf16[1,128,2048]{2,1,0:T(8,128)(2,1)}, u32[]{:S(2)}) copy-start(bf16[1,128,2048]{2,1,0:T(8,128)(2,1)} %k_ref.1) | copy-start | bytes 1572868
  4.1 1.0 %copy-start.2 = (bf16[1,128,2048]{2,1,0:T(8,128)(2,1)S(1)}, bf16[1,128,2048]{2,1,0:T(8,128)(2,1)}, u32[]{:S(2)}) copy-start(bf16[1,128,2048]{2,1,0:T(8,128)(2,1)} %v_ref.1) | copy-start | bytes 1572868
  5.1 1.0 %copy-start.3 = (bf16[1,128,2048]{2,1,0:T(8,128)(2,1)S(1)}, bf16[1,128,2048]{2,1,0:T(8,128)(2,1)}, u32[]{:S(2)}) copy-start(bf16[1,128,2048]{2,1,0:T(8,128)(2,1)} %u_ref.1) | copy-start | bytes 1572868

commit v2 on v1

--- a/solution.py
+++ b/solution.py
@@ -11,7 +11,7 @@
 HEADS = 16
 BLK = 128
 CORES = 2
-LEAD = 2
+LEAD = 1
 HIDDEN = -1e30
 MESH = pl.DeviceIdType.MESH
 
@@ -59,6 +59,7 @@
     fa_recv,
     ou_send,
     ou_recv,
+    lo_sem,
 ):
     chips = count // CORES
     heads = HEADS // CORES
@@ -123,10 +124,15 @@
             me + CORES,
         )
 
+    def down_rows(hop):
+        if hop > hops:
+            return rows(1, 1)
+        return rows(2, 1) if hop == hops - 1 else hop_rows(hop)
+
     def down(h, hop):
         return remote(
-            snd.at[:, hop_rows(hop), cols(h)],
-            rcv.at[:, hop_rows(hop), cols(h)],
+            snd.at[:, down_rows(hop), cols(h)],
+            rcv.at[:, down_rows(hop), cols(h)],
             dn_send.at[hop - 1, h],
             dn_recv.at[hop - 1, h],
             sec,
@@ -183,6 +189,13 @@
             sibling,
         )
 
+    def own(x):
+        dst = qb.at[rows(core), :] if x == 0 else kvw.at[x - 1, rows(reach + core), :]
+        return pltpu.make_async_copy(inputs[x].at[0, :, half(core)], dst, lo_sem.at[x])
+
+    def own_far():
+        return pltpu.make_async_copy(far_ref, fart.at[pl.ds(place * held, held)], lo_sem.at[3])
+
     barrier = pltpu.get_barrier_semaphore()
     for step in range(1, count):
         pl.semaphore_signal(
@@ -204,9 +217,12 @@
                 (2, height, heads * head_dim), kvw.dtype
             )
 
-    qb[rows(core), :] = q_ref[0, :, half(core)]
-    kvw[0, rows(reach + core), :] = k_ref[0, :, half(core)]
-    kvw[1, rows(reach + core), :] = v_ref[0, :, half(core)]
+    for x in range(3):
+        own(x).start()
+
+    @pl.when(side == core)
+    def _():
+        own_far().start()
 
     pl.semaphore_wait(barrier, count - 1 + 2 * CORES)
 
@@ -228,10 +244,6 @@
         @pl.when(jnp.logical_not(step * CORES + side == me))
         def _():
             spread(step, place).start()
-
-    @pl.when(side == core)
-    def _():
-        fart[pl.ds(place * held, held)] = far_ref[...]
 
     for x in range(3):
         swap(x, core).start()
@@ -251,7 +263,13 @@
             bias[pl.ds(qi * BLK, BLK), pl.ds(i * BLK, BLK)] = here + shown
 
     for x in range(3):
+        own(x).wait()
         swap(x, other).wait_recv()
+
+    @pl.when(side == core)
+    def _():
+        own_far().wait()
+
     for step in range(chips):
 
         @pl.when(jnp.logical_not(core * chips + step == me))
@@ -312,10 +330,12 @@
         results[x][0, :, cols(core * heads + h)] = st[x, rows(core), cols(h)]
 
     def send_down(h, hop):
-        @pl.when(chip >= hop)
+        @pl.when(chip >= (hops - 1 if hop > hops else hop))
         def _():
             for kv in range(2):
-                snd[kv, hop_rows(hop), cols(h)] = acc[h, kv, hop_rows(hop), :].astype(jnp.bfloat16)
+                snd[kv, down_rows(hop), cols(h)] = acc[h, kv, down_rows(hop), :].astype(
+                    jnp.bfloat16
+                )
             down(h, hop).start()
 
     def at(h, action):
@@ -347,6 +367,8 @@
             relay(h, 0, source).wait_recv()
         compute(h)
         send_down(h, hops)
+        if hops > 1:
+            send_down(h, hops + 1)
         for x in range(2):
             hand_out(h, x)
 
@@ -360,6 +382,8 @@
             @pl.when(jnp.logical_and(chip < chips - 1, chip + 1 >= hop))
             def _():
                 down(h, hop).wait_recv()
+                if hop == hops - 1:
+                    down(h, hops + 1).wait_recv()
                 for kv in range(2):
                     acc[h, kv, pl.ds(target * BLK, height), :] += rcv[
                         kv, hop_rows(hop), cols(h)
@@ -386,11 +410,12 @@
         def _():
             send_relay(i + LEAD + 1)
 
-        for hop in range(1, hops + 1):
+        for hop in range(1, hops):
             at(i - (hop - 1), arrive(hop))
-        at(i - (hops - 1), work)
         for hop in range(hops, 0, -1):
             at(i - (hops - 1) - 1 - (hops - hop), settle(hop))
+        at(i - (hops - 1), arrive(hops))
+        at(i - (hops - 1), work)
 
     for x in range(3):
         swap(x, core).wait_send()
@@ -419,12 +444,23 @@
             @pl.when(chip >= hop)
             def _():
                 down(h, hop).wait_send()
+                if hop == hops - 1:
+                    down(h, hops + 1).wait_send()
 
         for to_core in range(CORES):
             relay(h, to_core, core).wait_send()
         for x in range(4):
             give(h, x).wait_send()
             take(h, x).wait_recv()
+
+
+def store(*refs):
+    sems = refs[8]
+    copies = [pltpu.make_async_copy(refs[x], refs[4 + x], sems.at[x]) for x in range(4)]
+    for copy in copies:
+        copy.start()
+    for copy in copies:
+        copy.wait()
 
 
 def local(queries, key_states, value_states, upstream, layout, segments):
@@ -441,14 +477,16 @@
     distance = (jnp.arange(blocks, dtype=jnp.int32)[None, :, None] - plan + blocks) % blocks
     far = jnp.sum(jnp.where(distance >= 3, plan, 0), axis=-1)
     far = jnp.broadcast_to(far[:, :, None], (held, blocks, BLK)).astype(jnp.int32)
+    away = pl.BlockSpec(memory_space=pl.ANY)
     vmem = pl.BlockSpec(memory_space=pltpu.VMEM)
     part = heads * head_dim
     dma = pltpu.SemaphoreType.DMA
-    return tuple(
+    shapes = [jax.ShapeDtypeStruct(queries.shape, jnp.bfloat16)] * 4
+    made = tuple(
         pl.pallas_call(
             functools.partial(kernel, sections, count, head_dim),
-            out_shape=[jax.ShapeDtypeStruct(queries.shape, jnp.bfloat16)] * 4,
-            in_specs=[pl.BlockSpec(memory_space=pltpu.SMEM)] + [vmem] * 5,
+            out_shape=shapes,
+            in_specs=[pl.BlockSpec(memory_space=pltpu.SMEM)] + [away] * 5,
             out_specs=[vmem] * 4,
             scratch_shapes=[
                 pltpu.VMEM((2, (reach + 2) * BLK, part), jnp.bfloat16),
@@ -464,8 +502,8 @@
                 dma((CORES, 2, heads)),
                 dma((max(hops - 1, 1), heads)),
                 dma((max(hops - 1, 1), heads)),
-                dma((hops, heads)),
-                dma((hops, heads)),
+                dma((hops + 1, heads)),
+                dma((hops + 1, heads)),
                 dma((3,)),
                 dma((3,)),
                 dma((CORES, heads)),
@@ -474,11 +512,21 @@
                 dma((chips,)),
                 dma((4, heads)),
                 dma((4, heads)),
+                dma((4,)),
             ],
             compiler_params=pltpu.CompilerParams(
-                collective_id=0, has_side_effects=True, vmem_limit_bytes=44 * 1024 * 1024
+                collective_id=0, has_side_effects=True, vmem_limit_bytes=56 * 1024 * 1024
             ),
         )(segments, far, queries, key_states, value_states, upstream)
+    )
+    return tuple(
+        pl.pallas_call(
+            store,
+            out_shape=shapes,
+            in_specs=[vmem] * 4,
+            out_specs=[away] * 4,
+            scratch_shapes=[dma((4,))],
+        )(*made)
     )
 
 

time: 71.3 us -> 67 us (0.940)
  local copies, waits for them, and re-layouts: 7.99 us -> 0.67 us
  Pallas kernels: 61.6 us -> 64.7 us
    unnamed x14 -> x0, local copies, waits for them, and re-layouts: 7.92 us -> none
    pallas_call x0 -> x1, Pallas kernels: none -> 2.86 us  [local(): pl.pallas_call(store, out_shape=shapes, in_specs=[vmem] * 4, out_specs=[a...]
where the time goes in v2:
time: 67 us; the launch traced here: 66.8 us
  Pallas kernels  64.7 us (97%)
  other arithmetic  0.72 us (1%)
  local copies, waits for them, and re-layouts  0.67 us (1%)
    pallas_call x1, Pallas kernels, local(): pl.pallas_call(functools.partial(kernel, sections, count, head_dim), out_...  61.9 us
    pallas_call x1, Pallas kernels, local(): pl.pallas_call(store, out_shape=shapes, in_specs=[vmem] * 4, out_specs=[a...  2.86 us

profile of v2, /device:TPU:0, one launch (start us, length us, event | category | flops | bytes accessed | tf_op | source)
XLA Modules:
  0.0 66.8 jit_solution(9810900327379432371)
XLA Ops:
  0.6 0.7 %fusion.3 = s32[2,8]{1,0:T(2,128)S(1)} fusion(s32[1,2,8,4]{2,3,1,0:T(4,128)} %param.10), kind=kLoop, calls=%fused_computation.8 | loop fusion | flops 1008 | bytes 320 | tf_op jit(solution)/shard_map/reduce_sum | solution.py:478
  1.3 0.7 %broadcast_in_dim.4.far_ref = s32[2,8,128]{2,1,0:T(8,128)} broadcast(s32[2,8]{1,0:T(2,128)S(1)} %fusion.3), dimensions={0,1} | broadcast | bytes 8256 | tf_op jit(solution)/shard_map/broadcast_in_dim | solution.py:479
  2.0 61.9 %shard_map.93 = (bf16[1,128,2048]{2,1,0:T(8,128)(2,1)}, bf16[1,128,2048]{2,1,0:T(8,128)(2,1)}, bf16[1,128,2048]{2,1,0:T(8,128)(2,1)}, bf16[1,128,2048]{2,1,0:T(8,128)(2,1)}) custom-call(s32[1,8]{1,0:T(1,128)} %seg_ref.1, s32[2,8,128]{2,1,0:T(8,128)} %broadcast_in_dim.4.far_ref, bf16[1,128,2048]{2,1,0:T(8,128)(2,1)} %q_ref.1, bf16[1,128,2048]{2,1,0:T(8,128)(2,1)} %k_ref.1, ...), custom_call_target="tpu_custom_call" | custom-call | tf_op jit(solution)/shard_map/pallas_call | solution.py:486
  63.9 2.9 %shard_map.94 = (bf16[1,128,2048]{2,1,0:T(8,128)(2,1)}, bf16[1,128,2048]{2,1,0:T(8,128)(2,1)}, bf16[1,128,2048]{2,1,0:T(8,128)(2,1)}, bf16[1,128,2048]{2,1,0:T(8,128)(2,1)}) custom-call(bf16[1,128,2048]{2,1,0:T(8,128)(2,1)} %get-tuple-element.8.refs_0_, bf16[1,128,2048]{2,1,0:T(8,128)(2,1)} %get-tuple-element.9.refs_1_, ...), custom_call_target="tpu_custom_call" | custom-call | tf_op jit(solution)/shard_map/pallas_call | solution.py:523

commit v3 on v2

--- a/solution.py
+++ b/solution.py
@@ -523,7 +523,7 @@
         pl.pallas_call(
             store,
             out_shape=shapes,
-            in_specs=[vmem] * 4,
+            in_specs=[away] * 4,
             out_specs=[away] * 4,
             scratch_shapes=[dma((4,))],
         )(*made)

time: 67 us -> 129 us (1.93)
  Pallas kernels: 64.7 us -> 127 us
    pallas_call x1, Pallas kernels: 2.86 us -> 64.7 us  [local(): pl.pallas_call(store, out_shape=shapes, in_specs=[away] * 4, out_specs=[a...]
where the time goes in v3:
time: 129 us
  Pallas kernels  127 us (98%)
    pallas_call x1, Pallas kernels, local(): pl.pallas_call(store, out_shape=shapes, in_specs=[away] * 4, out_specs=[a...  64.7 us
    pallas_call x1, Pallas kernels, local(): pl.pallas_call(functools.partial(kernel, sections, count, head_dim), out_...  61.9 us

profile of v3, /device:TPU:0, one launch (start us, length us, event | category | flops | bytes accessed | tf_op | source)
XLA Modules:
  0.0 128.6 jit_solution(11861932942394870572)
XLA Ops:
  0.6 0.7 fusion.3
  1.3 0.7 broadcast_in_dim.4.far_ref
  2.0 61.9 %shard_map.93 = (bf16[1,128,2048]{2,1,0:T(8,128)(2,1)}, bf16[1,128,2048]{2,1,0:T(8,128)(2,1)}, bf16[1,128,2048]{2,1,0:T(8,128)(2,1)}, bf16[1,128,2048]{2,1,0:T(8,128)(2,1)}) custom-call(s32[1,8]{1,0:T(1,128)} %seg_ref.1, s32[2,8,128]{2,1,0:T(8,128)} %broadcast_in_dim.4.far_ref, bf16[1,128,2048]{2,1,0:T(8,128)(2,1)} %q_ref.1, bf16[1,128,2048]{2,1,0:T(8,128)(2,1)} %k_ref.1, ...), custom_call_target="tpu_custom_call" | custom-call | tf_op jit(solution)/shard_map/pallas_call | solution.py:486
  63.9 64.7 %shard_map.94 = (bf16[1,128,2048]{2,1,0:T(8,128)(2,1)}, bf16[1,128,2048]{2,1,0:T(8,128)(2,1)}, bf16[1,128,2048]{2,1,0:T(8,128)(2,1)}, bf16[1,128,2048]{2,1,0:T(8,128)(2,1)}) custom-call(bf16[1,128,2048]{2,1,0:T(8,128)(2,1)} %get-tuple-element.8.refs_0_, bf16[1,128,2048]{2,1,0:T(8,128)(2,1)} %get-tuple-element.9.refs_1_, ...), custom_call_target="tpu_custom_call" | custom-call | tf_op jit(solution)/shard_map/pallas_call | solution.py:523
